TPU v7x, 1024 devices: a whole 4x8x16 slice. The times are simulated.
1024 devices in a mesh: section: 8 (over z_hi, core), expert: 32 (over y, z_lo), dp: 4 (over x).
Axes of the slice: x: 4, y: 8, z: 16 (z_hi: 4, z_lo: 4; z = z_hi * 4 + z_lo), core: 2. Of those that a mesh axis runs over, the one named last changes fastest.
Arguments:
- tokens: bfloat16 [16384, 2048], P(('dp', 'expert')), parts along dimension 0, may hold values from -6 to 6
- routes: int32 [16384, 2], P(('dp', 'expert')), parts along dimension 0, may hold values from 0 to 63, all different within a row; in each aligned block of 128 rows (0 to 127, 128 to 255, ...) at most 8 rows name the same one
- gates: bfloat16 [16384, 2], P(('dp', 'expert')), parts along dimension 0, may hold values from 0.19921875 to 1
- fc_in: bfloat16 [64, 2048, 4096], P('expert', None, 'section'), may hold values from -0.125 to 0.125
- fc_out: bfloat16 [64, 4096, 2048], P('expert', 'section'), may hold values from -0.09375 to 0.09375
- norm_gain: float32 [2048], replicated, may hold values from 0.5 to 1.5
- norm_bias: float32 [2048], replicated, may hold values from -3 to 3
- key_weight: bfloat16 [2048, 1024], P(None, 'section'), may hold values from -0.125 to 0.125
- value_weight: bfloat16 [2048, 1024], P(None, 'section'), may hold values from -0.125 to 0.125
- queries: bfloat16 [16384, 1024], P(('dp', 'expert'), 'section'), parts along dimension 0, may hold values from -160 to 160
- source_len: int32 [128], P(('dp', 'expert')), parts along dimension 0, may hold values from 32 to 128
- target_len: int32 [128], P(('dp', 'expert')), parts along dimension 0, may hold values from 32 to 128
Outputs:
- context: bfloat16 [16384, 1024], P(('dp', 'expert'), 'section'), parts along dimension 0
There are 4 independent parts, one for each index of `dp`. A program takes and returns all parts, laid end to end along the dimension named above; an argument that names none is the same for every part. Nothing has to cross between parts.
Inputs may be any that keep to these rules, and one draw needn't show every extreme that they name: `routes`: each row names two different experts. The 128 rows of one index of expert name one expert at most 8 times, a bound that some block reaches.
All inputs are finite; a program needn't handle non-finite values.
Results may differ from a plain program's by a relative error of at most 0.04.
Values may be sent and summed in bfloat16 or wider, within the bound.
A program may use at most 64 MiB of HBM per device.

v0:
```python
import jax
import jax.numpy as jnp
from jax import lax
from jax.sharding import PartitionSpec as P

HEAD_DIM = 128
SRC = 128
TGT = 128


def normalize(summed, norm_gain, norm_bias):
    center = summed - jnp.mean(summed, axis=-1, keepdims=True)
    spread = jnp.mean(center * center, axis=-1, keepdims=True)
    return (center * lax.rsqrt(spread + 1e-05) * norm_gain + norm_bias).astype(jnp.bfloat16)


def expert_parts(arrived, fc_in, fc_out):
    hidden = jax.nn.relu(
        jnp.einsum("gecd,edf->gecf", arrived, fc_in, preferred_element_type=jnp.float32)
    ).astype(jnp.bfloat16)
    return jnp.einsum("gecf,efd->gecd", hidden, fc_out, preferred_element_type=jnp.float32).astype(
        jnp.bfloat16
    )


def shards(
    tokens,
    routes,
    gates,
    fc_in,
    fc_out,
    norm_gain,
    norm_bias,
    key_weight,
    value_weight,
    queries,
    source_len,
    target_len,
):
    tok_rows, width = tokens.shape
    exp_local = fc_in.shape[0]
    groups = lax.axis_size("expert")
    experts = exp_local * groups
    capacity = max(2, 4 * tok_rows // experts)
    slot_count = experts * capacity
    pair_ids = routes.reshape(-1)
    onehot = (pair_ids[:, None] == jnp.arange(experts, dtype=jnp.int32)[None, :]).astype(jnp.int32)
    order_rank = jnp.sum((jnp.cumsum(onehot, axis=0) - onehot) * onehot, axis=1)
    slot_index = pair_ids * capacity + order_rank
    select = slot_index[:, None] == jnp.arange(slot_count, dtype=jnp.int32)[None, :]
    placing = jnp.sum(select.astype(jnp.bfloat16).reshape(tok_rows, 2, slot_count), axis=1)
    gate_flat = gates.reshape(-1)[:, None]
    combining = jnp.sum(
        jnp.where(select, gate_flat, jnp.zeros_like(gate_flat)).reshape(tok_rows, 2, slot_count),
        axis=1,
    )
    outgoing = jnp.einsum("ts,td->sd", placing, tokens, preferred_element_type=jnp.float32).astype(
        jnp.bfloat16
    )
    outgoing = outgoing.reshape(groups, exp_local * capacity, width)
    arrived = lax.all_to_all(outgoing, "expert", split_axis=0, concat_axis=0, tiled=True)
    partial_value = expert_parts(arrived.reshape(groups, exp_local, capacity, width), fc_in, fc_out)
    returned = lax.all_to_all(
        partial_value.reshape(groups, exp_local * capacity, width),
        "expert",
        split_axis=0,
        concat_axis=0,
        tiled=True,
    )
    mixed = jnp.dot(
        combining, returned.reshape(slot_count, width), preferred_element_type=jnp.float32
    )
    summed = lax.psum(mixed, "section")
    memory = normalize(tokens.astype(jnp.float32) + summed, norm_gain, norm_bias)
    key_rows = jnp.dot(memory, key_weight, preferred_element_type=jnp.float32).astype(jnp.bfloat16)
    value_rows = jnp.dot(memory, value_weight, preferred_element_type=jnp.float32).astype(
        jnp.bfloat16
    )
    sentences = tok_rows // SRC
    heads_here = key_weight.shape[1] // HEAD_DIM
    query_grid = queries.reshape(sentences, TGT, heads_here, HEAD_DIM)
    key_grid = key_rows.reshape(sentences, SRC, heads_here, HEAD_DIM)
    value_grid = value_rows.reshape(sentences, SRC, heads_here, HEAD_DIM)
    scores = jnp.einsum(
        "sqhd,skhd->shqk", query_grid, key_grid, preferred_element_type=jnp.float32
    ) * HEAD_DIM ** (-0.5)
    key_mask = jnp.arange(SRC, dtype=jnp.int32)[None, :] < source_len[:, None]
    scores = jnp.where(key_mask[:, None, None, :], scores, -jnp.inf)
    highest = jnp.max(scores, axis=-1, keepdims=True)
    expo = jnp.exp(scores - highest)
    weights = (expo / jnp.sum(expo, axis=-1, keepdims=True)).astype(jnp.bfloat16)
    context = jnp.einsum("shqk,skhd->sqhd", weights, value_grid, preferred_element_type=jnp.float32)
    row_mask = jnp.arange(TGT, dtype=jnp.int32)[None, :] < target_len[:, None]
    context = jnp.where(row_mask[:, :, None, None], context, 0.0)
    return context.reshape(sentences * TGT, heads_here * HEAD_DIM).astype(jnp.bfloat16)


def solution(mesh):
    in_specs = (
        P(("dp", "expert"), None),
        P(("dp", "expert"), None),
        P(("dp", "expert"), None),
        P("expert", None, "section"),
        P("expert", "section", None),
        P(),
        P(),
        P(None, "section"),
        P(None, "section"),
        P(("dp", "expert"), "section"),
        P(("dp", "expert")),
        P(("dp", "expert")),
    )
    out_specs = P(("dp", "expert"), "section")
    return jax.shard_map(shards, mesh=mesh, in_specs=in_specs, out_specs=out_specs, check_vma=False)
```

profile of v0, /device:TPU:1, one launch (start us, length us, event | category | flops | bytes accessed | tf_op | source)
XLA Modules:
  0.0 269.7 jit_solution(10543082996294118046)
XLA Ops:
  6.5 0.0 copy-start
  6.5 0.0 all-reduce.2.cloned.1.call-start
  6.5 0.8 copy.41
  7.4 0.1 eq.40
  7.5 0.1 eq.44
  7.7 0.6 reduce-window.6
  8.3 0.2 slice_reduce_fusion
  8.5 0.1 fusion.41
  8.6 0.1 reduce_sum.63
  8.8 0.1 copy.44
  8.8 0.7 multiply_add_fusion
  9.5 0.8 fusion.38
  10.4 1.8 convolution_convert_fusion
  12.2 63.9 %all_to_all.10 = bf16[32,16,2048]{2,1,0:T(8,128)(2,1)S(1)} all-to-all(bf16[32,16,2048]{2,1,0:T(8,128)(2,1)S(1)} %bitcast.83), channel_id=1, replica_groups=mesh['section'=8,'expert'=32,'dp'=4] {'expert'}, dimensions={0} | all-to-all | bytes 4194304 | tf_op jit(solution)/shard_map/all_to_all | solution.py:61
  76.0 7.2 %fusion.7 = bf16[32,2,8,2048]{3,2,0,1:T(8,128)(2,1)} fusion(bf16[2,512,2048]{2,1,0:T(8,128)(2,1)} %param.16, bf16[2,2048,512]{2,1,0:T(8,128)(2,1)} %param.15, bf16[32,16,2048]{2,1,0:T(8,128)(2,1)S(1)} %all_to_all.10), kind=kOutput, calls=%fused_computation.6 | convolution fusion | flops 2149056512 | bytes 12582912 | tf_op jit(solution)/shard_map/gecf,efd->gecd/dot_general | solution.py:21
  83.2 1.7 copy.63
  84.9 54.7 %all_to_all.11 = bf16[32,16,2048]{2,1,0:T(8,128)(2,1)S(1)} all-to-all(bf16[32,16,2048]{2,1,0:T(8,128)(2,1)S(1)} %bitcast.84), channel_id=1, replica_groups=mesh['section'=8,'expert'=32,'dp'=4] {'expert'}, dimensions={0} | all-to-all | bytes 4194304 | tf_op jit(solution)/shard_map/all_to_all | solution.py:63
  139.7 1.5 fusion.48
  141.1 0.0 all-reduce.2.cloned.1.call-update
  142.5 116.5 %all-reduce.2.cloned.1.call-done = f32[128,2048]{1,0:T(8,128)} async-done(((f32[128,2048]{1,0:T(8,128)}), f32[128,2048]{1,0:T(8,128)}) %all-reduce.2.cloned.1.call-update) | async-done | bytes 1048592 | tf_op jit(solution)/shard_map/psum | solution.py:73
  259.0 0.0 copy-done.2
  259.0 1.5 fusion.36
  260.5 0.0 copy-done.1
  260.5 0.3 multiply_reduce_fusion
  260.8 0.0 copy-done.5
  260.8 0.0 copy-done.6
  260.8 0.3 add_convert_fusion
  261.1 0.0 copy-done
  261.1 0.1 copy-done.4
  261.2 0.4 fusion.47
  261.7 0.5 fusion.29
  262.2 0.7 copy.47
  (15 shorter events, 0.1 us)
Async XLA Ops:
  6.5 254.6 %copy-start = (bf16[2048,128]{1,0:T(8,128)(2,1)S(1)}, bf16[2048,128]{1,0:T(8,128)(2,1)}, u32[]{:S(2)}) copy-start(bf16[2048,128]{1,0:T(8,128)(2,1)} %param.19) | copy-start | bytes 1572868
  6.5 252.4 %all-reduce.2.cloned.1.call-start = ((), (), s32[]{:S(2)}) async-start(), calls=%async_computation.2 | async-start | bytes 2097152 | tf_op jit(solution)/shard_map/psum | solution.py:73
  139.6 119.3 %copy-start.2 = (bf16[128,2048]{1,0:T(8,128)(2,1)S(1)}, bf16[128,2048]{1,0:T(8,128)(2,1)}, u32[]{:S(2)}) copy-start(bf16[128,2048]{1,0:T(8,128)(2,1)} %param.12) | copy-start | bytes 1572868
  141.1 119.7 %copy-start.5 = (f32[2048]{0:T(1024)S(1)}, f32[2048]{0:T(1024)}, u32[]{:S(2)}) copy-start(f32[2048]{0:T(1024)} %param.18) | copy-start | bytes 24580
  141.1 119.7 %copy-start.6 = (f32[2048]{0:T(1024)S(1)}, f32[2048]{0:T(1024)}, u32[]{:S(2)}) copy-start(f32[2048]{0:T(1024)} %param.17) | copy-start | bytes 24580
  259.0 1.5 copy-start.1
  260.5 0.8 copy-start.4
  260.5 1.2 copy-start.3
Sparse Core Ops, SparseCore 0:
  141.3 117.6 all-reduce.1
where the time goes:
time: 270 us
  blocking collectives  119 us (44%)
  waiting for transfers between devices  116 us (43%)
  between operations  14.8 us (5%)
  matrix products  11.3 us (4%)
  other arithmetic  4.44 us (2%)
  local copies, waits for them, and re-layouts  4.11 us (2%)
    psum x1, waiting for transfers between devices, shards(): summed = lax.psum(mixed, 'section')  116 us
    all_to_all x1, blocking collectives, shards(): lax.all_to_all(outgoing, 'expert', split_axis=0, concat_axis=0, tiled=True)  63.9 us
    all_to_all x1, blocking collectives, shards(): lax.all_to_all(partial_value.reshape(groups, exp_local * capacity, width)...  54.7 us
    dot_general x1, matrix products, expert_parts(): jnp.einsum('gecf,efd->gecd', hidden, fc_out, preferred_element_type=jnp.f...  7.15 us
  transfers between devices with their start and end apart: 1, of which 1 were waited for; matrix products, arithmetic and copies ran while one was open for 0% of the time, Pallas kernels for 0%

commit v1 on v0

v1 whole, which is shorter than its diff:
```python
import functools

import jax
import jax.numpy as jnp
from jax import lax
from jax.experimental import pallas as pl
from jax.experimental.pallas import tpu as pltpu
from jax.sharding import PartitionSpec as P

MESH = pl.DeviceIdType.MESH
BF16, F32 = jnp.bfloat16, jnp.float32

HEAD_DIM = 128
ROWS = 128
D = 2048
HALF = 1024
HID = 512
CAP = 8
NY, NZ, NLO = 8, 16, 4
NCH, CW = 2, 512
FIRST = 5
SETS = ((0, FIRST), (FIRST, NY))


def dy_of(m):
    return ((m + 1) // 2) * (1 - 2 * ((m + 1) % 2))


def mirror(m):
    return jnp.where((m == 0) | (m == 7), m, m + 1 - 2 * ((m + 1) % 2))


def dz_of(d, core):
    return d - 4 * ((d + core) // 3)


def kernel(
    tokens, routes, gates, fc_in, fc_out, gain, bias, key_w, value_w, queries, source_len, target_len,
    context,
    outgoing, arrived, rows_in, w_in, w_out, kw, vw, hidden, part, returned, combining,
    mixed_f, mixed_b, scattered, gathered,
    load_sem, disp_s, disp_r, fwd_s, fwd_r, swap_s, swap_r, hid_s, hid_r,
    ret_s, ret_r, rs_s, rs_r, ag_s, ag_r, sib_s, sib_r,
):
    section, group = lax.axis_index("section"), lax.axis_index("expert")
    zhi, core = section // 2, section % 2
    y, zlo = group // NLO, group % NLO
    z = zhi * NLO + zlo
    other = 1 - core

    def device(y2, z2, core2):
        return {"section": (z2 // NLO) * 2 + core2, "expert": y2 * NLO + z2 % NLO}

    def to(m, d):
        return device((y + dy_of(m) + NY) % NY, (z + dz_of(d, core) + NZ) % NZ, core)

    def to_hi(r):
        return device(y, (z + NLO * r) % NZ, core)

    sibling = device(y, z, other)

    loads = [
        pltpu.make_async_copy(fc_in, w_in, load_sem.at[0]),
        pltpu.make_async_copy(
            fc_out.at[:, :, pl.ds(pl.multiple_of(core * HALF, HALF), HALF)], w_out.at[core], load_sem.at[1]
        ),
        pltpu.make_async_copy(key_w, kw, load_sem.at[2]),
        pltpu.make_async_copy(value_w, vw, load_sem.at[3]),
    ]
    for load in loads:
        load.start()

    barrier = pltpu.get_barrier_semaphore()

    def greet(k, carry):
        m, d = k // NLO, k % NLO
        source = device((y - dy_of(m) + NY) % NY, (z - dz_of(d, core) + NZ) % NZ, core)
        pl.semaphore_signal(barrier, inc=1, device_id=source, device_id_type=MESH)
        return carry

    lax.fori_loop(1, NY * NLO, greet, 0)
    for r in range(1, 4):
        pl.semaphore_signal(barrier, inc=1, device_id=to_hi(r), device_id_type=MESH)
    pl.semaphore_signal(barrier, inc=1, device_id=sibling, device_id_type=MESH)

    experts = 2 * NY * NLO
    lane = lax.broadcasted_iota(jnp.int32, (ROWS, experts), 1)
    route0, route1 = routes[:, 0:1], routes[:, 1:2]
    hot0 = jnp.where(lane == route0, 1.0, 0.0)
    hot1 = jnp.where(lane == route1, 1.0, 0.0)
    earlier = jnp.where(
        lax.broadcasted_iota(jnp.int32, (ROWS, ROWS), 0) > lax.broadcasted_iota(jnp.int32, (ROWS, ROWS), 1),
        1.0, 0.0,
    )
    before = jnp.dot(earlier.astype(BF16), (hot0 + hot1).astype(BF16), preferred_element_type=F32)
    slot0 = route0.astype(F32) * CAP + jnp.sum(before * hot0, axis=1, keepdims=True)
    slot1 = route1.astype(F32) * CAP + jnp.sum(before * hot1, axis=1, keepdims=True)
    slots = experts * CAP
    column = lax.broadcasted_iota(jnp.int32, (1, slots), 1)
    m_col = column // (NLO * 2 * CAP)
    d_col = (column // (2 * CAP)) % NLO
    y_col = (y + dy_of(m_col) + NY) % NY
    group_col = y_col * NLO + (zlo + d_col) % NLO
    slot_col = (group_col * (2 * CAP) + column % (2 * CAP)).astype(F32)
    pick0, pick1 = slot0 == slot_col, slot1 == slot_col
    placing = jnp.where(pick0 | pick1, 1.0, 0.0)
    gate0, gate1 = gates[:, 0:1].astype(F32), gates[:, 1:2].astype(F32)
    combining[...] = (jnp.where(pick0, gate0, 0.0) + jnp.where(pick1, gate1, 0.0)).astype(BF16)
    half = tokens[:, pl.ds(pl.multiple_of(core * HALF, HALF), HALF)]
    placed = jnp.dot(placing.T.astype(BF16), half, preferred_element_type=F32).astype(BF16)
    outgoing[...] = placed.reshape(NY, NLO, 2 * CAP, HALF)

    pl.semaphore_wait(barrier, NY * NLO - 1 + 3 + 1)

    def dispatch_copy(m, d):
        return pltpu.make_async_remote_copy(
            src_ref=outgoing.at[m, d],
            dst_ref=arrived.at[core, mirror(m), (NLO - d) % NLO],
            send_sem=disp_s.at[m],
            recv_sem=disp_r.at[mirror(m)],
            device_id=to(m, d),
            device_id_type=MESH,
        )

    def send_dispatch(k, carry):
        dispatch_copy(k // NLO, k % NLO).start()
        return carry

    lax.fori_loop(1, NY * NLO, send_dispatch, 0)
    w_swap = pltpu.make_async_remote_copy(
        src_ref=fc_out.at[:, :, pl.ds(pl.multiple_of(other * HALF, HALF), HALF)],
        dst_ref=w_out.at[core],
        send_sem=swap_s,
        recv_sem=swap_r,
        device_id=sibling,
        device_id_type=MESH,
    )
    arrived[core, 0, 0] = outgoing[0, 0]

    def wait_bytes(ref, sem):
        pltpu.make_async_copy(ref, ref, sem).wait()

    def forward_copy(m):
        return pltpu.make_async_remote_copy(
            src_ref=arrived.at[core, m],
            dst_ref=arrived.at[core, m],
            send_sem=fwd_s.at[m],
            recv_sem=fwd_r.at[m],
            device_id=sibling,
            device_id_type=MESH,
        )

    def hidden_copy(number):
        m0, m1 = SETS[number]
        rows = pl.ds(m0 * NLO * CAP, (m1 - m0) * NLO * CAP)
        return pltpu.make_async_remote_copy(
            src_ref=hidden.at[core, :, rows],
            dst_ref=hidden.at[core, :, rows],
            send_sem=hid_s.at[number],
            recv_sem=hid_r.at[number],
            device_id=sibling,
            device_id_type=MESH,
        )

    def return_copy(ch, m, d):
        return pltpu.make_async_remote_copy(
            src_ref=part.at[ch, m, d],
            dst_ref=returned.at[ch, mirror(m), (NLO - d) % NLO],
            send_sem=ret_s.at[ch, m],
            recv_sem=ret_r.at[ch, mirror(m)],
            device_id=to(m, d),
            device_id_type=MESH,
        )

    w_swap_started = False
    for number, (m0, m1) in enumerate(SETS):
        def take(m, carry):
            wait_bytes(arrived.at[core, m], disp_r.at[m])
            forward_copy(m).start()
            return carry

        if m0 == 0:
            wait_bytes(arrived.at[core, 0, pl.ds(1, NLO - 1)], disp_r.at[0])
            forward_copy(0).start()
        lax.fori_loop(max(m0, 1), m1, take, 0)
        if number == 0:
            w_swap.start()

        def relayout(m, carry):
            wait_bytes(arrived.at[other, m], fwd_r.at[m])
            for h in range(2):
                block = arrived[h, m].astype(F32)
                for i in range(2):
                    rows_in[i, pl.ds(pl.multiple_of(m * NLO * CAP, NLO * CAP), NLO * CAP), h * HALF:(h + 1) * HALF] = (
                        block[:, i * CAP:(i + 1) * CAP, :].reshape(NLO * CAP, HALF).astype(BF16)
                    )
            return carry

        lax.fori_loop(m0, m1, relayout, 0)
        first, count = m0 * NLO * CAP, (m1 - m0) * NLO * CAP
        if number == 0:
            loads[0].wait()
        for i in range(2):
            for n in range(0, HID, 256):
                h = jnp.dot(rows_in[i, first:first + count, :], w_in[i, :, n:n + 256], preferred_element_type=F32)
                hidden[core, i, first:first + count, n:n + 256] = jnp.maximum(h, 0.0).astype(BF16)
        hidden_copy(number).start()
        if number == 0:
            loads[1].wait()
            w_swap.wait()
        hidden_copy(number).wait()
        for ch in range(NCH):
            cols = slice(ch * CW, (ch + 1) * CW)
            sums = [
                jnp.dot(hidden[0, i, first:first + count, :], w_out[0, i, :, cols], preferred_element_type=F32)
                + jnp.dot(hidden[1, i, first:first + count, :], w_out[1, i, :, cols], preferred_element_type=F32)
                for i in range(2)
            ]
            sums = [s.reshape((m1 - m0) * NLO, CAP, CW) for s in sums]
            both = jnp.concatenate(sums, axis=1).astype(BF16)
            part[ch, m0:m1] = both.reshape(m1 - m0, NLO, 2 * CAP, CW)

            def send_return(k, carry):
                return_copy(ch, k // NLO, k % NLO).start()
                return carry

            lax.fori_loop(max(m0 * NLO, 1), m1 * NLO, send_return, 0)
            if m0 == 0:
                returned[ch, 0, 0] = part[ch, 0, 0]

    def scatter_copy(ch, r):
        return pltpu.make_async_remote_copy(
            src_ref=mixed_b.at[ch, (zhi + r) % 4],
            dst_ref=scattered.at[ch, r - 1],
            send_sem=rs_s.at[ch, r - 1],
            recv_sem=rs_r.at[ch, r - 1],
            device_id=to_hi(r),
            device_id_type=MESH,
        )

    def gather_copy(ch, r):
        return pltpu.make_async_remote_copy(
            src_ref=gathered.at[ch, core, zhi],
            dst_ref=gathered.at[ch, core, zhi],
            send_sem=ag_s.at[ch, r - 1],
            recv_sem=ag_r.at[ch, r - 1],
            device_id=to_hi(r),
            device_id_type=MESH,
        )

    def share_copy(ch):
        return pltpu.make_async_remote_copy(
            src_ref=gathered.at[ch, core],
            dst_ref=gathered.at[ch, core],
            send_sem=sib_s.at[ch],
            recv_sem=sib_r.at[ch],
            device_id=sibling,
            device_id_type=MESH,
        )

    quarter = ROWS // 4
    for ch in range(NCH):
        def wait_return(m, carry):
            wait_bytes(returned.at[ch, m], ret_r.at[ch, m])
            return carry

        wait_bytes(returned.at[ch, 0, pl.ds(1, NLO - 1)], ret_r.at[ch, 0])
        lax.fori_loop(1, NY, wait_return, 0)
        mixed = jnp.dot(combining[...], returned[ch].reshape(slots, CW), preferred_element_type=F32)
        mixed = mixed.reshape(4, quarter, CW)
        mixed_f[ch] = mixed
        mixed_b[ch] = mixed.astype(BF16)
        for r in range(1, 4):
            scatter_copy(ch, r).start()
        for r in range(1, 4):
            scatter_copy(ch, r).wait_recv()
        total = mixed_f[ch, zhi]
        for r in range(3):
            total = total + scattered[ch, r].astype(F32)
        gathered[ch, core, zhi] = total.astype(BF16)
        for r in range(1, 4):
            gather_copy(ch, r).start()
    for ch in range(NCH):
        for r in range(1, 4):
            gather_copy(ch, r).wait()
        share_copy(ch).start()
    for ch in range(NCH):
        share_copy(ch).wait()

    blocks = [(h, ch) for h in range(2) for ch in range(NCH)]
    spans = [slice(h * HALF + ch * CW, h * HALF + (ch + 1) * CW) for h, ch in blocks]
    summed = [
        tokens[:, span].astype(F32) + gathered[ch, h].reshape(ROWS, CW).astype(F32)
        for (h, ch), span in zip(blocks, spans)
    ]
    mean = sum(jnp.sum(s, axis=1, keepdims=True) for s in summed) / D
    centered = [s - mean for s in summed]
    spread = sum(jnp.sum(s * s, axis=1, keepdims=True) for s in centered) / D
    scale = lax.rsqrt(spread + 1e-05)
    loads[2].wait()
    loads[3].wait()
    keys = values = jnp.zeros((ROWS, HEAD_DIM), F32)
    for block, span in zip(centered, spans):
        memory = (block * scale * gain[:, span] + bias[:, span]).astype(BF16)
        keys = keys + jnp.dot(memory, kw[span, :], preferred_element_type=F32)
        values = values + jnp.dot(memory, vw[span, :], preferred_element_type=F32)
    keys, values = keys.astype(BF16), values.astype(BF16)
    scores = lax.dot_general(queries[...], keys, (((1,), (1,)), ((), ())), preferred_element_type=F32)
    scores = scores * HEAD_DIM ** (-0.5)
    position = lax.broadcasted_iota(jnp.int32, (ROWS, ROWS), 1)
    scores = jnp.where(position < source_len[0], scores, -jnp.inf)
    expo = jnp.exp(scores - jnp.max(scores, axis=1, keepdims=True))
    weights = (expo / jnp.sum(expo, axis=1, keepdims=True)).astype(BF16)
    result = jnp.dot(weights, values, preferred_element_type=F32)
    row = lax.broadcasted_iota(jnp.int32, (ROWS, HEAD_DIM), 0)
    context[...] = jnp.where(row < target_len[0], result, 0.0).astype(BF16)

    wait_bytes(outgoing.at[0, pl.ds(1, NLO - 1)], disp_s.at[0])
    for ch in range(NCH):
        wait_bytes(part.at[ch, 0, pl.ds(1, NLO - 1)], ret_s.at[ch, 0])

    def drain(m, carry):
        wait_bytes(outgoing.at[m], disp_s.at[m])
        for ch in range(NCH):
            wait_bytes(part.at[ch, m], ret_s.at[ch, m])
        return carry

    lax.fori_loop(1, NY, drain, 0)

    def drain_forward(m, carry):
        wait_bytes(arrived.at[core, m], fwd_s.at[m])
        return carry

    lax.fori_loop(0, NY, drain_forward, 0)
    for ch in range(NCH):
        for r in range(1, 4):
            scatter_copy(ch, r).wait_send()


def shards(
    tokens, routes, gates, fc_in, fc_out, norm_gain, norm_bias, key_weight, value_weight, queries,
    source_len, target_len,
):
    vmem = pl.BlockSpec(memory_space=pltpu.VMEM)
    smem = pl.BlockSpec(memory_space=pltpu.SMEM)
    hbm = pl.BlockSpec(memory_space=pl.ANY)
    dma = pltpu.SemaphoreType.DMA
    return pl.pallas_call(
        kernel,
        out_shape=jax.ShapeDtypeStruct((ROWS, HEAD_DIM), BF16),
        in_specs=[vmem, vmem, vmem, hbm, hbm, vmem, vmem, hbm, hbm, vmem, smem, smem],
        out_specs=vmem,
        scratch_shapes=[
            pltpu.VMEM((NY, NLO, 2 * CAP, HALF), BF16),
            pltpu.VMEM((2, NY, NLO, 2 * CAP, HALF), BF16),
            pltpu.VMEM((2, NY * NLO * CAP, D), BF16),
            pltpu.VMEM((2, D, HID), BF16),
            pltpu.VMEM((2, 2, HID, HALF), BF16),
            pltpu.VMEM((D, HEAD_DIM), BF16),
            pltpu.VMEM((D, HEAD_DIM), BF16),
            pltpu.VMEM((2, 2, NY * NLO * CAP, HID), BF16),
            pltpu.VMEM((NCH, NY, NLO, 2 * CAP, CW), BF16),
            pltpu.VMEM((NCH, NY, NLO, 2 * CAP, CW), BF16),
            pltpu.VMEM((ROWS, NY * NLO * 2 * CAP), BF16),
            pltpu.VMEM((NCH, 4, ROWS // 4, CW), F32),
            pltpu.VMEM((NCH, 4, ROWS // 4, CW), BF16),
            pltpu.VMEM((NCH, 3, ROWS // 4, CW), BF16),
            pltpu.VMEM((NCH, 2, 4, ROWS // 4, CW), BF16),
            dma((4,)),
            dma((NY,)), dma((NY,)),
            dma((NY,)), dma((NY,)),
            dma, dma,
            dma((2,)), dma((2,)),
            dma((NCH, NY)), dma((NCH, NY)),
            dma((NCH, 3)), dma((NCH, 3)),
            dma((NCH, 3)), dma((NCH, 3)),
            dma((NCH,)), dma((NCH,)),
        ],
        compiler_params=pltpu.CompilerParams(
            collective_id=0, has_side_effects=True, vmem_limit_bytes=56 * 2**20
        ),
        cost_estimate=pl.CostEstimate(flops=2_300_000_000, bytes_accessed=10_000_000, transcendentals=20_000),
    )(
        tokens, routes, gates, fc_in, fc_out, norm_gain.reshape(1, -1), norm_bias.reshape(1, -1),
        key_weight, value_weight, queries, source_len, target_len,
    )


def solution(mesh):
    in_specs = (
        P(("dp", "expert"), None),
        P(("dp", "expert"), None),
        P(("dp", "expert"), None),
        P("expert", None, "section"),
        P("expert", "section", None),
        P(),
        P(),
        P(None, "section"),
        P(None, "section"),
        P(("dp", "expert"), "section"),
        P(("dp", "expert")),
        P(("dp", "expert")),
    )
    out_specs = P(("dp", "expert"), "section")
    return jax.shard_map(shards, mesh=mesh, in_specs=in_specs, out_specs=out_specs, check_vma=False)
```

time: 270 us -> 135 us (0.50)
  the two profiles are of different devices: /device:TPU:1 before, /device:TPU:25 now
where the time goes in v1:
time: 135 us
  Pallas kernels  129 us (96%)
  local copies, waits for them, and re-layouts  4.16 us (3%)
    pallas_call x1, Pallas kernels, shards(): pl.pallas_call(kernel, out_shape=jax.ShapeDtypeStruct((ROWS, HEAD_DIM), B...  129 us
    unnamed x3, local copies, waits for them, and re-layouts  4.16 us

profile of v1, /device:TPU:25, one launch (start us, length us, event | category | flops | bytes accessed | tf_op | source)
XLA Modules:
  0.0 134.5 jit_solution(3208561818026945544)
XLA Ops:
  1.3 1.4 %copy.14.gates = bf16[128,2]{1,0:T(8,128)(2,1)} copy(bf16[128,2]{0,1:T(2,128)(2,1)} %param.14) | data formatting | bytes 1024 | tf_op args[2]
  2.7 1.4 %copy.13.routes = s32[128,2]{1,0:T(8,128)} copy(s32[128,2]{0,1:T(2,128)} %param.13) | data formatting | bytes 2048 | tf_op args[1]
  4.1 129.1 %shard_map.118 = bf16[128,128]{1,0:T(8,128)(2,1)} custom-call(bf16[128,2048]{1,0:T(8,128)(2,1)} %tokens.1, s32[128,2]{1,0:T(8,128)} %copy.13.routes, bf16[128,2]{1,0:T(8,128)(2,1)} %copy.14.gates, bf16[2,2048,512]{2,1,0:T(8,128)(2,1)} %fc_in.1, bf16[2,512,2048]{2,1,0:T(8,128)(2,1)} %fc_out.1, f32[1,2048]{1,0:T(1,128)} %bitcast.2, f32[1,2048]{1,0:T(1,128)} %bitcast.3, ...), custom_call_target="tpu_custom_call" | custom-call | flops 2300000000 | bytes 10000000 | tf_op jit(solution)/shard_map/pallas_call | solution.py:348
  133.2 1.4 %copy.18 = bf16[128,128]{1,0:T(8,128)(2,1)} copy(bf16[128,128]{1,0:T(8,128)(2,1)} %shard_map.118) | data formatting | bytes 65536

commit v2 on v1

v2 whole, which is shorter than its diff:
```python
import functools

import jax
import jax.numpy as jnp
from jax import lax
from jax.experimental import pallas as pl
from jax.experimental.pallas import tpu as pltpu
from jax.sharding import PartitionSpec as P

MESH = pl.DeviceIdType.MESH
BF16, F32 = jnp.bfloat16, jnp.float32

HEAD_DIM = 128
ROWS = 128
D = 2048
HALF = 1024
HID = 512
CAP = 8
NY, NZ, NLO = 8, 16, 4
NCH, CW = 2, 512
FIRST = 5
PEERS = NY * NLO
SLOT = 2 * CAP
NEAR, FAR = 0, 1
SETS = ((0, FIRST), (FIRST, NY))
MOVED = ((1, FIRST * NLO), (FIRST * NLO, PEERS))
HOLD = 1


def dy_of(m):
    return ((m + 1) // 2) * (1 - 2 * ((m + 1) % 2))


def mirror(m):
    return jnp.where((m == 0) | (m == 7), m, m + 1 - 2 * ((m + 1) % 2))


def dz_of(d, core):
    return d - 4 * ((d + core) // 3)


def kernel(
    tokens, routes, gates, fc_in, fc_out, gain, bias, key_w, value_w, queries, source_len, target_len,
    context,
    outgoing, arrived, rows_in, w_in, w_out, kv, hidden, part, returned, combining,
    mixed_f, mixed_b, scattered, gathered,
    load_sem, disp_s, disp_r, fwd_s, fwd_r, swap_s, swap_r, hid_s, hid_r,
    ret_s, ret_r, rs_s, rs_r, ag_s, ag_r, sib_s, sib_r,
):
    section, group = lax.axis_index("section"), lax.axis_index("expert")
    zhi, core = section // 2, section % 2
    y, zlo = group // NLO, group % NLO
    z = zhi * NLO + zlo
    other = 1 - core

    def device(y2, z2, core2):
        return {"section": (z2 // NLO) * 2 + core2, "expert": y2 * NLO + z2 % NLO}

    def to(m, d):
        return device((y + dy_of(m) + NY) % NY, (z + dz_of(d, core) + NZ) % NZ, core)

    def to_hi(r):
        return device(y, (z + NLO * r) % NZ, core)

    sibling = device(y, z, other)

    loads = [
        pltpu.make_async_copy(fc_in, w_in, load_sem.at[0]),
        pltpu.make_async_copy(
            fc_out.at[:, :, pl.ds(pl.multiple_of(core * HALF, HALF), HALF)], w_out.at[core], load_sem.at[1]
        ),
        pltpu.make_async_copy(key_w, kv.at[:, 0:HEAD_DIM], load_sem.at[2]),
        pltpu.make_async_copy(value_w, kv.at[:, HEAD_DIM:2 * HEAD_DIM], load_sem.at[3]),
    ]
    for load in loads:
        load.start()

    barrier = pltpu.get_barrier_semaphore()

    def greet(k, carry):
        m, d = k // NLO, k % NLO
        source = device((y - dy_of(m) + NY) % NY, (z - dz_of(d, core) + NZ) % NZ, core)
        pl.semaphore_signal(barrier, inc=1, device_id=source, device_id_type=MESH)
        return carry

    lax.fori_loop(1, PEERS, greet, 0)
    for r in range(1, 4):
        pl.semaphore_signal(barrier, inc=1, device_id=to_hi(r), device_id_type=MESH)
    pl.semaphore_signal(barrier, inc=1, device_id=sibling, device_id_type=MESH)

    experts, slots = 2 * PEERS, PEERS * SLOT
    expert_id = lax.broadcasted_iota(jnp.int32, (experts, ROWS), 0)
    route0, route1 = routes[0:1, :], routes[1:2, :]
    hot0 = jnp.where(expert_id == route0, 1.0, 0.0)
    hot1 = jnp.where(expert_id == route1, 1.0, 0.0)
    earlier = jnp.where(
        lax.broadcasted_iota(jnp.int32, (ROWS, ROWS), 0) < lax.broadcasted_iota(jnp.int32, (ROWS, ROWS), 1),
        1.0, 0.0,
    )
    before = jnp.dot((hot0 + hot1).astype(BF16), earlier.astype(BF16), preferred_element_type=F32)
    slot0 = route0 * CAP + jnp.sum(before * hot0, axis=0, keepdims=True).astype(jnp.int32)
    slot1 = route1 * CAP + jnp.sum(before * hot1, axis=0, keepdims=True).astype(jnp.int32)

    def picks(first, count):
        row = lax.broadcasted_iota(jnp.int32, (count, ROWS), 0) + first
        m_row, d_row = row // (NLO * SLOT), (row // SLOT) % NLO
        group_row = ((y + dy_of(m_row) + NY) % NY) * NLO + (zlo + d_row) % NLO
        slot_row = group_row * SLOT + row % SLOT
        return slot0 == slot_row, slot1 == slot_row

    half = tokens[:, pl.ds(pl.multiple_of(core * HALF, HALF), HALF)]

    def place(pick0, pick1, m0, m1):
        placing = jnp.where(pick0 | pick1, 1.0, 0.0).astype(BF16)
        placed = jnp.dot(placing, half, preferred_element_type=F32).astype(BF16)
        outgoing[m0 * NLO:m1 * NLO] = placed.reshape((m1 - m0) * NLO, SLOT, HALF)

    def combine_matrix(pick0, pick1):
        gate0, gate1 = gates[0:1, :].astype(F32), gates[1:2, :].astype(F32)
        return (jnp.where(pick0, gate0, 0.0) + jnp.where(pick1, gate1, 0.0)).T.astype(BF16)

    def mirrored(k):
        m, d = k // NLO, k % NLO
        return mirror(m) * NLO + (NLO - d) % NLO

    def wait_bytes(ref, sem):
        pltpu.make_async_copy(ref, ref, sem).wait()

    def moved(ref, number):
        first, end = MOVED[number]
        return ref.at[pl.ds(first, end - first)]

    def dispatch_copy(k, number):
        return pltpu.make_async_remote_copy(
            src_ref=outgoing.at[k],
            dst_ref=arrived.at[core, mirrored(k)],
            send_sem=disp_s.at[number],
            recv_sem=disp_r.at[mirror(k // NLO)],
            device_id=to(k // NLO, k % NLO),
            device_id_type=MESH,
        )

    def send_dispatch(number):
        def send(k, carry):
            dispatch_copy(k, number).start()
            return carry

        lax.fori_loop(*MOVED[number], send, 0)

    near = picks(0, FIRST * NLO * SLOT)
    place(*near, 0, FIRST)
    pl.semaphore_wait(barrier, PEERS - 1 + 3 + 1)
    send_dispatch(NEAR)
    w_swap = pltpu.make_async_remote_copy(
        src_ref=fc_out.at[:, :, pl.ds(pl.multiple_of(other * HALF, HALF), HALF)],
        dst_ref=w_out.at[core],
        send_sem=swap_s,
        recv_sem=swap_r,
        device_id=sibling,
        device_id_type=MESH,
    )
    w_swap.start()
    arrived[core, 0] = outgoing[0]
    far = picks(FIRST * NLO * SLOT, (NY - FIRST) * NLO * SLOT)
    place(*far, FIRST, NY)
    wait_bytes(moved(outgoing, NEAR), disp_s.at[NEAR])
    send_dispatch(FAR)
    combining[:, :FIRST * NLO * SLOT] = combine_matrix(*near)
    combining[:, FIRST * NLO * SLOT:] = combine_matrix(*far)

    def forward_copy(m):
        blocks = pl.ds(m * NLO, NLO)
        return pltpu.make_async_remote_copy(
            src_ref=arrived.at[core, blocks],
            dst_ref=arrived.at[core, blocks],
            send_sem=fwd_s.at[m],
            recv_sem=fwd_r.at[m],
            device_id=sibling,
            device_id_type=MESH,
        )

    def hidden_copy(number):
        m0, m1 = SETS[number]
        rows = pl.ds(m0 * NLO * CAP, (m1 - m0) * NLO * CAP)
        return pltpu.make_async_remote_copy(
            src_ref=hidden.at[core, :, rows],
            dst_ref=hidden.at[core, :, rows],
            send_sem=hid_s.at[number],
            recv_sem=hid_r.at[number],
            device_id=sibling,
            device_id_type=MESH,
        )

    def make_hidden(number):
        m0, m1 = SETS[number]

        def take(m, carry):
            wait_bytes(arrived.at[core, pl.ds(m * NLO, NLO)], disp_r.at[m])
            forward_copy(m).start()
            return carry

        if m0 == 0:
            wait_bytes(arrived.at[core, pl.ds(1, NLO - 1)], disp_r.at[0])
            forward_copy(0).start()
        lax.fori_loop(max(m0, 1), m1, take, 0)

        def relayout(m, carry):
            wait_bytes(arrived.at[other, pl.ds(m * NLO, NLO)], fwd_r.at[m])
            for h in range(2):
                block = arrived[h, pl.ds(m * NLO, NLO)].astype(F32)
                for i in range(2):
                    rows_in[i, pl.ds(pl.multiple_of(m * NLO * CAP, NLO * CAP), NLO * CAP), h * HALF:(h + 1) * HALF] = (
                        block[:, i * CAP:(i + 1) * CAP, :].reshape(NLO * CAP, HALF).astype(BF16)
                    )
            return carry

        lax.fori_loop(m0, m1, relayout, 0)
        rows = slice(m0 * NLO * CAP, m1 * NLO * CAP)
        if number == NEAR:
            loads[0].wait()
        for i in range(2):
            for n in range(0, HID, 256):
                h = jnp.dot(rows_in[i, rows, :], w_in[i, :, n:n + 256], preferred_element_type=F32)
                hidden[core, i, rows, n:n + 256] = jnp.maximum(h, 0.0).astype(BF16)
        hidden_copy(number).start()
        if number == NEAR:
            loads[1].wait()
            w_swap.wait()
        hidden_copy(number).wait()

    def expert_outputs(m0, m1, ch):
        rows, cols = slice(m0 * NLO * CAP, m1 * NLO * CAP), slice(ch * CW, (ch + 1) * CW)
        sums = [
            jnp.dot(hidden[0, i, rows, :], w_out[0, i, :, cols], preferred_element_type=F32)
            + jnp.dot(hidden[1, i, rows, :], w_out[1, i, :, cols], preferred_element_type=F32)
            for i in range(2)
        ]
        sums = [s.reshape((m1 - m0) * NLO, CAP, CW) for s in sums]
        return jnp.concatenate(sums, axis=1).astype(BF16)

    def return_copy(ch, k, number):
        return pltpu.make_async_remote_copy(
            src_ref=part.at[ch, k],
            dst_ref=returned.at[ch, mirrored(k)],
            send_sem=ret_s.at[ch, number],
            recv_sem=ret_r.at[ch, number],
            device_id=to(k // NLO, k % NLO),
            device_id_type=MESH,
        )

    units = []

    def settle(left):
        while len(units) > left:
            ch, number = units.pop(0)
            wait_bytes(moved(part.at[ch], number), ret_s.at[ch, number])

    def send_back(ch, number):
        m0, m1 = SETS[number]
        part[ch, m0 * NLO:m1 * NLO] = expert_outputs(m0, m1, ch)
        settle(HOLD - 1)

        def send(k, carry):
            return_copy(ch, k, number).start()
            return carry

        lax.fori_loop(*MOVED[number], send, 0)
        units.append((ch, number))
        if number == NEAR:
            returned[ch, 0] = part[ch, 0]

    def scatter_copy(ch, r):
        return pltpu.make_async_remote_copy(
            src_ref=mixed_b.at[ch, (zhi + r) % 4],
            dst_ref=scattered.at[ch, r - 1],
            send_sem=rs_s.at[ch, r - 1],
            recv_sem=rs_r.at[ch, r - 1],
            device_id=to_hi(r),
            device_id_type=MESH,
        )

    def gather_copy(ch, r):
        return pltpu.make_async_remote_copy(
            src_ref=gathered.at[ch, core, zhi],
            dst_ref=gathered.at[ch, core, zhi],
            send_sem=ag_s.at[ch, r - 1],
            recv_sem=ag_r.at[ch, r - 1],
            device_id=to_hi(r),
            device_id_type=MESH,
        )

    def share_copy(ch):
        return pltpu.make_async_remote_copy(
            src_ref=gathered.at[ch, core],
            dst_ref=gathered.at[ch, core],
            send_sem=sib_s.at[ch],
            recv_sem=sib_r.at[ch],
            device_id=sibling,
            device_id_type=MESH,
        )

    quarter = ROWS // 4

    def scatter(ch):
        for number in (FAR, NEAR):
            wait_bytes(moved(returned.at[ch], number), ret_r.at[ch, number])
        mixed = jnp.dot(combining[...], returned[ch].reshape(slots, CW), preferred_element_type=F32)
        mixed = mixed.reshape(4, quarter, CW)
        mixed_f[ch] = mixed
        mixed_b[ch] = mixed.astype(BF16)
        for r in (2, 1, 3):
            scatter_copy(ch, r).start()

    def gather(ch):
        for r in range(1, 4):
            scatter_copy(ch, r).wait_recv()
        total = mixed_f[ch, zhi]
        for r in range(3):
            total = total + scattered[ch, r].astype(F32)
        gathered[ch, core, zhi] = total.astype(BF16)
        for r in (2, 1, 3):
            gather_copy(ch, r).start()

    def share(ch):
        for r in range(1, 4):
            gather_copy(ch, r).wait()
        share_copy(ch).start()

    make_hidden(NEAR)
    wait_bytes(moved(outgoing, FAR), disp_s.at[FAR])
    send_back(0, NEAR)
    make_hidden(FAR)
    send_back(0, FAR)
    send_back(1, NEAR)
    scatter(0)
    send_back(1, FAR)
    gather(0)
    scatter(1)
    share(0)
    gather(1)
    share(1)
    settle(0)
    for ch in range(NCH):
        share_copy(ch).wait()

    blocks = [(h, ch) for h in range(2) for ch in range(NCH)]
    spans = [slice(h * HALF + ch * CW, h * HALF + (ch + 1) * CW) for h, ch in blocks]
    summed = [
        tokens[:, span].astype(F32) + gathered[ch, h].reshape(ROWS, CW).astype(F32)
        for (h, ch), span in zip(blocks, spans)
    ]
    mean = sum(jnp.sum(s, axis=1, keepdims=True) for s in summed) / D
    centered = [s - mean for s in summed]
    spread = sum(jnp.sum(s * s, axis=1, keepdims=True) for s in centered) / D
    scale = lax.rsqrt(spread + 1e-05)
    loads[2].wait()
    loads[3].wait()
    both = jnp.zeros((ROWS, 2 * HEAD_DIM), F32)
    for block, span in zip(centered, spans):
        memory = (block * scale * gain[:, span] + bias[:, span]).astype(BF16)
        both = both + jnp.dot(memory, kv[span, :], preferred_element_type=F32)
    keys, values = both[:, :HEAD_DIM].astype(BF16), both[:, HEAD_DIM:].astype(BF16)
    scores = lax.dot_general(queries[...], keys, (((1,), (1,)), ((), ())), preferred_element_type=F32)
    scores = scores * HEAD_DIM ** (-0.5)
    position = lax.broadcasted_iota(jnp.int32, (ROWS, ROWS), 1)
    scores = jnp.where(position < source_len[0], scores, -jnp.inf)
    expo = jnp.exp(scores - jnp.max(scores, axis=1, keepdims=True))
    weights = (expo / jnp.sum(expo, axis=1, keepdims=True)).astype(BF16)
    result = jnp.dot(weights, values, preferred_element_type=F32)
    row = lax.broadcasted_iota(jnp.int32, (ROWS, HEAD_DIM), 0)
    context[...] = jnp.where(row < target_len[0], result, 0.0).astype(BF16)

    def drain_forward(m, carry):
        wait_bytes(arrived.at[core, pl.ds(m * NLO, NLO)], fwd_s.at[m])
        return carry

    lax.fori_loop(0, NY, drain_forward, 0)
    for ch in range(NCH):
        for r in range(1, 4):
            scatter_copy(ch, r).wait_send()


def shards(
    tokens, routes, gates, fc_in, fc_out, norm_gain, norm_bias, key_weight, value_weight, queries,
    source_len, target_len,
):
    vmem = pl.BlockSpec(memory_space=pltpu.VMEM)
    smem = pl.BlockSpec(memory_space=pltpu.SMEM)
    hbm = pl.BlockSpec(memory_space=pl.ANY)
    dma = pltpu.SemaphoreType.DMA
    return pl.pallas_call(
        kernel,
        out_shape=jax.ShapeDtypeStruct((ROWS, HEAD_DIM), BF16),
        in_specs=[vmem, vmem, vmem, hbm, hbm, vmem, vmem, hbm, hbm, vmem, smem, smem],
        out_specs=vmem,
        scratch_shapes=[
            pltpu.VMEM((PEERS, SLOT, HALF), BF16),
            pltpu.VMEM((2, PEERS, SLOT, HALF), BF16),
            pltpu.VMEM((2, PEERS * CAP, D), BF16),
            pltpu.VMEM((2, D, HID), BF16),
            pltpu.VMEM((2, 2, HID, HALF), BF16),
            pltpu.VMEM((D, 2 * HEAD_DIM), BF16),
            pltpu.VMEM((2, 2, PEERS * CAP, HID), BF16),
            pltpu.VMEM((NCH, PEERS, SLOT, CW), BF16),
            pltpu.VMEM((NCH, PEERS, SLOT, CW), BF16),
            pltpu.VMEM((ROWS, PEERS * SLOT), BF16),
            pltpu.VMEM((NCH, 4, ROWS // 4, CW), F32),
            pltpu.VMEM((NCH, 4, ROWS // 4, CW), BF16),
            pltpu.VMEM((NCH, 3, ROWS // 4, CW), BF16),
            pltpu.VMEM((NCH, 2, 4, ROWS // 4, CW), BF16),
            dma((4,)),
            dma((2,)), dma((NY,)),
            dma((NY,)), dma((NY,)),
            dma, dma,
            dma((2,)), dma((2,)),
            dma((NCH, 2)), dma((NCH, 2)),
            dma((NCH, 3)), dma((NCH, 3)),
            dma((NCH, 3)), dma((NCH, 3)),
            dma((NCH,)), dma((NCH,)),
        ],
        compiler_params=pltpu.CompilerParams(
            collective_id=0, has_side_effects=True, vmem_limit_bytes=56 * 2**20
        ),
        cost_estimate=pl.CostEstimate(flops=2_300_000_000, bytes_accessed=10_000_000, transcendentals=20_000),
    )(
        tokens, routes.T, gates.T, fc_in, fc_out, norm_gain.reshape(1, -1), norm_bias.reshape(1, -1),
        key_weight, value_weight, queries, source_len, target_len,
    )


def solution(mesh):
    in_specs = (
        P(("dp", "expert"), None),
        P(("dp", "expert"), None),
        P(("dp", "expert"), None),
        P("expert", None, "section"),
        P("expert", "section", None),
        P(),
        P(),
        P(None, "section"),
        P(None, "section"),
        P(("dp", "expert"), "section"),
        P(("dp", "expert")),
        P(("dp", "expert")),
    )
    out_specs = P(("dp", "expert"), "section")
    return jax.shard_map(shards, mesh=mesh, in_specs=in_specs, out_specs=out_specs, check_vma=False)
```

time: 135 us -> 124 us (0.919)
  the two profiles are of different devices: /device:TPU:25 before, /device:TPU:185 now
where the time goes in v2:
time: 124 us
  Pallas kernels  121 us (98%)
  local copies, waits for them, and re-layouts  1.38 us (1%)
  between operations  1.3 us (1%)
    pallas_call x1, Pallas kernels, shards(): pl.pallas_call(kernel, out_shape=jax.ShapeDtypeStruct((ROWS, HEAD_DIM), B...  121 us

profile of v2, /device:TPU:185, one launch (start us, length us, event | category | flops | bytes accessed | tf_op | source)
XLA Modules:
  0.0 124.0 jit_solution(11419240233723269727)
XLA Ops:
  1.3 121.3 %shard_map.118 = bf16[128,128]{1,0:T(8,128)(2,1)} custom-call(bf16[128,2048]{1,0:T(8,128)(2,1)} %tokens.1, s32[2,128]{1,0:T(2,128)} %bitcast.6, bf16[2,128]{1,0:T(2,128)(2,1)} %bitcast.7, bf16[2,2048,512]{2,1,0:T(8,128)(2,1)} %fc_in.1, bf16[2,512,2048]{2,1,0:T(8,128)(2,1)} %fc_out.1, f32[1,2048]{1,0:T(1,128)} %bitcast.4, f32[1,2048]{1,0:T(1,128)} %bitcast.5, ...), custom_call_target="tpu_custom_call" | custom-call | flops 2300000000 | bytes 10000000 | tf_op jit(solution)/shard_map/pallas_call | solution.py:391
  122.6 1.4 %copy.16 = bf16[128,128]{1,0:T(8,128)(2,1)} copy(bf16[128,128]{1,0:T(8,128)(2,1)} %shard_map.118) | data formatting | bytes 65536

commit v3 on v2

--- a/solution.py
+++ b/solution.py
@@ -40,8 +40,9 @@
 
 
 def kernel(
-    tokens, routes, gates, fc_in, fc_out, gain, bias, key_w, value_w, queries, source_len, target_len,
+    tokens_h, routes, gates, fc_in, fc_out, gain_h, bias_h, key_w, value_w, queries_h, source_len, target_len,
     context,
+    tokens, gain, bias, queries,
     outgoing, arrived, rows_in, w_in, w_out, kv, hidden, part, returned, combining,
     mixed_f, mixed_b, scattered, gathered,
     load_sem, disp_s, disp_r, fwd_s, fwd_r, swap_s, swap_r, hid_s, hid_r,
@@ -64,16 +65,19 @@
 
     sibling = device(y, z, other)
 
+    tokens_load = pltpu.make_async_copy(tokens_h, tokens, load_sem.at[4])
+    tokens_load.start()
     loads = [
-        pltpu.make_async_copy(fc_in, w_in, load_sem.at[0]),
+        pltpu.make_async_copy(fc_in, w_in.at[core], load_sem.at[0]),
         pltpu.make_async_copy(
             fc_out.at[:, :, pl.ds(pl.multiple_of(core * HALF, HALF), HALF)], w_out.at[core], load_sem.at[1]
         ),
         pltpu.make_async_copy(key_w, kv.at[:, 0:HEAD_DIM], load_sem.at[2]),
         pltpu.make_async_copy(value_w, kv.at[:, HEAD_DIM:2 * HEAD_DIM], load_sem.at[3]),
+        pltpu.make_async_copy(gain_h, gain, load_sem.at[5]),
+        pltpu.make_async_copy(bias_h, bias, load_sem.at[6]),
+        pltpu.make_async_copy(queries_h, queries, load_sem.at[7]),
     ]
-    for load in loads:
-        load.start()
 
     barrier = pltpu.get_barrier_semaphore()
 
@@ -108,6 +112,9 @@
         slot_row = group_row * SLOT + row % SLOT
         return slot0 == slot_row, slot1 == slot_row
 
+    for load in loads:
+        load.start()
+    tokens_load.wait()
     half = tokens[:, pl.ds(pl.multiple_of(core * HALF, HALF), HALF)]
 
     def place(pick0, pick1, m0, m1):
@@ -159,6 +166,15 @@
         device_id=sibling,
         device_id_type=MESH,
     )
+    in_swap = pltpu.make_async_remote_copy(
+        src_ref=fc_in,
+        dst_ref=w_in.at[core],
+        send_sem=hid_s,
+        recv_sem=hid_r,
+        device_id=sibling,
+        device_id_type=MESH,
+    )
+    in_swap.start()
     w_swap.start()
     arrived[core, 0] = outgoing[0]
     far = picks(FIRST * NLO * SLOT, (NY - FIRST) * NLO * SLOT)
@@ -175,18 +191,6 @@
             dst_ref=arrived.at[core, blocks],
             send_sem=fwd_s.at[m],
             recv_sem=fwd_r.at[m],
-            device_id=sibling,
-            device_id_type=MESH,
-        )
-
-    def hidden_copy(number):
-        m0, m1 = SETS[number]
-        rows = pl.ds(m0 * NLO * CAP, (m1 - m0) * NLO * CAP)
-        return pltpu.make_async_remote_copy(
-            src_ref=hidden.at[core, :, rows],
-            dst_ref=hidden.at[core, :, rows],
-            send_sem=hid_s.at[number],
-            recv_sem=hid_r.at[number],
             device_id=sibling,
             device_id_type=MESH,
         )
@@ -218,15 +222,15 @@
         rows = slice(m0 * NLO * CAP, m1 * NLO * CAP)
         if number == NEAR:
             loads[0].wait()
-        for i in range(2):
-            for n in range(0, HID, 256):
-                h = jnp.dot(rows_in[i, rows, :], w_in[i, :, n:n + 256], preferred_element_type=F32)
-                hidden[core, i, rows, n:n + 256] = jnp.maximum(h, 0.0).astype(BF16)
-        hidden_copy(number).start()
+            in_swap.wait()
+        for sec in range(2):
+            for i in range(2):
+                for n in range(0, HID, 256):
+                    h = jnp.dot(rows_in[i, rows, :], w_in[sec, i, :, n:n + 256], preferred_element_type=F32)
+                    hidden[sec, i, rows, n:n + 256] = jnp.maximum(h, 0.0).astype(BF16)
         if number == NEAR:
             loads[1].wait()
             w_swap.wait()
-        hidden_copy(number).wait()
 
     def expert_outputs(m0, m1, ch):
         rows, cols = slice(m0 * NLO * CAP, m1 * NLO * CAP), slice(ch * CW, (ch + 1) * CW)
@@ -353,8 +357,8 @@
     centered = [s - mean for s in summed]
     spread = sum(jnp.sum(s * s, axis=1, keepdims=True) for s in centered) / D
     scale = lax.rsqrt(spread + 1e-05)
-    loads[2].wait()
-    loads[3].wait()
+    for load in loads[2:]:
+        load.wait()
     both = jnp.zeros((ROWS, 2 * HEAD_DIM), F32)
     for block, span in zip(centered, spans):
         memory = (block * scale * gain[:, span] + bias[:, span]).astype(BF16)
@@ -391,13 +395,17 @@
     return pl.pallas_call(
         kernel,
         out_shape=jax.ShapeDtypeStruct((ROWS, HEAD_DIM), BF16),
-        in_specs=[vmem, vmem, vmem, hbm, hbm, vmem, vmem, hbm, hbm, vmem, smem, smem],
+        in_specs=[hbm, vmem, vmem, hbm, hbm, hbm, hbm, hbm, hbm, hbm, smem, smem],
         out_specs=vmem,
         scratch_shapes=[
+            pltpu.VMEM((ROWS, D), BF16),
+            pltpu.VMEM((1, D), F32),
+            pltpu.VMEM((1, D), F32),
+            pltpu.VMEM((ROWS, HEAD_DIM), BF16),
             pltpu.VMEM((PEERS, SLOT, HALF), BF16),
             pltpu.VMEM((2, PEERS, SLOT, HALF), BF16),
             pltpu.VMEM((2, PEERS * CAP, D), BF16),
-            pltpu.VMEM((2, D, HID), BF16),
+            pltpu.VMEM((2, 2, D, HID), BF16),
             pltpu.VMEM((2, 2, HID, HALF), BF16),
             pltpu.VMEM((D, 2 * HEAD_DIM), BF16),
             pltpu.VMEM((2, 2, PEERS * CAP, HID), BF16),
@@ -408,11 +416,11 @@
             pltpu.VMEM((NCH, 4, ROWS // 4, CW), BF16),
             pltpu.VMEM((NCH, 3, ROWS // 4, CW), BF16),
             pltpu.VMEM((NCH, 2, 4, ROWS // 4, CW), BF16),
-            dma((4,)),
+            dma((8,)),
             dma((2,)), dma((NY,)),
             dma((NY,)), dma((NY,)),
             dma, dma,
-            dma((2,)), dma((2,)),
+            dma, dma,
             dma((NCH, 2)), dma((NCH, 2)),
             dma((NCH, 3)), dma((NCH, 3)),
             dma((NCH, 3)), dma((NCH, 3)),

time: 124 us -> 122 us (0.984)
  the two profiles are of different devices: /device:TPU:185 before, /device:TPU:31 now
where the time goes in v3:
time: 122 us
  Pallas kernels  119 us (98%)
  local copies, waits for them, and re-layouts  1.38 us (1%)
  between operations  1.3 us (1%)
    pallas_call x1, Pallas kernels, shards(): pl.pallas_call(kernel, out_shape=jax.ShapeDtypeStruct((ROWS, HEAD_DIM), B...  119 us

profile of v3, /device:TPU:31, one launch (start us, length us, event | category | flops | bytes accessed | tf_op | source)
XLA Modules:
  0.0 122.2 jit_solution(12766190943528830478)
XLA Ops:
  1.3 119.5 %shard_map.118 = bf16[128,128]{1,0:T(8,128)(2,1)} custom-call(bf16[128,2048]{1,0:T(8,128)(2,1)} %tokens_h.1, s32[2,128]{1,0:T(2,128)} %bitcast.6, bf16[2,128]{1,0:T(2,128)(2,1)} %bitcast.7, bf16[2,2048,512]{2,1,0:T(8,128)(2,1)} %fc_in.1, bf16[2,512,2048]{2,1,0:T(8,128)(2,1)} %fc_out.1, f32[1,2048]{1,0:T(1,128)} %bitcast.4, f32[1,2048]{1,0:T(1,128)} %bitcast.5, ...), custom_call_target="tpu_custom_call" | custom-call | flops 2300000000 | bytes 10000000 | tf_op jit(solution)/shard_map/pallas_call | solution.py:395
  120.8 1.4 %copy.16 = bf16[128,128]{1,0:T(8,128)(2,1)} copy(bf16[128,128]{1,0:T(8,128)(2,1)} %shard_map.118) | data formatting | bytes 65536

commit v4 on v3

--- a/solution.py
+++ b/solution.py
@@ -149,7 +149,8 @@
 
     def send_dispatch(number):
         def send(k, carry):
-            dispatch_copy(k, number).start()
+            first, end = MOVED[number]
+            dispatch_copy(first + end - 1 - k, number).start()
             return carry
 
         lax.fori_loop(*MOVED[number], send, 0)

time: 122 us -> 114 us (0.934)
  the two profiles are of different devices: /device:TPU:31 before, /device:TPU:117 now
where the time goes in v4:
time: 114 us; the launch traced here: 113 us
  Pallas kernels  111 us (97%)
  local copies, waits for them, and re-layouts  1.38 us (1%)
  between operations  1.3 us (1%)
    pallas_call x1, Pallas kernels, shards(): pl.pallas_call(kernel, out_shape=jax.ShapeDtypeStruct((ROWS, HEAD_DIM), B...  111 us

profile of v4, /device:TPU:117, one launch (start us, length us, event | category | flops | bytes accessed | tf_op | source)
XLA Modules:
  0.0 113.5 jit_solution(11902788337978444529)
XLA Ops:
  1.3 110.8 %shard_map.118 = bf16[128,128]{1,0:T(8,128)(2,1)} custom-call(bf16[128,2048]{1,0:T(8,128)(2,1)} %tokens_h.1, s32[2,128]{1,0:T(2,128)} %bitcast.6, bf16[2,128]{1,0:T(2,128)(2,1)} %bitcast.7, bf16[2,2048,512]{2,1,0:T(8,128)(2,1)} %fc_in.1, bf16[2,512,2048]{2,1,0:T(8,128)(2,1)} %fc_out.1, f32[1,2048]{1,0:T(1,128)} %bitcast.4, f32[1,2048]{1,0:T(1,128)} %bitcast.5, ...), custom_call_target="tpu_custom_call" | custom-call | flops 2300000000 | bytes 10000000 | tf_op jit(solution)/shard_map/pallas_call | solution.py:396
  112.1 1.4 %copy.16 = bf16[128,128]{1,0:T(8,128)(2,1)} copy(bf16[128,128]{1,0:T(8,128)(2,1)} %shard_map.118) | data formatting | bytes 65536
